TPU v7x, 512 devices: a whole 4x4x16 slice. The times are simulated.
512 devices in a mesh: context: 64 (over x, z), tensor: 8 (over y, core).
Axes of the slice: x: 4, y: 4, z: 16, core: 2. Of those that a mesh axis runs over, the one named last changes fastest.
Arguments:
- query: bfloat16 [8192, 2048], P('context', 'tensor'), may hold values from -5 to 5
- key_proj: bfloat16 [8192, 1024], P('context', 'tensor'), may hold values from -5 to 5
- value: bfloat16 [8192, 1024], P('context', 'tensor'), may hold values from -6 to 6
- out_weight: bfloat16 [2048, 4096], P('tensor'), may hold values from -0.125 to 0.125
- grad_out: bfloat16 [8192, 4096], P('context', 'tensor'), may hold values from -6 to 6
- order: int32 [8192], replicated, may hold values from 0 to 8191, each once
- segment: int32 [8192], replicated, may hold values from 0 to 7, never falling along the last dimension, each value on 1 to 2048 neighbouring positions
Outputs:
- output: bfloat16 [8192, 4096], P('context', 'tensor')
- grad_query: bfloat16 [8192, 2048], P('context', 'tensor')
- grad_key: bfloat16 [8192, 1024], P('context', 'tensor')
- grad_value: bfloat16 [8192, 1024], P('context', 'tensor')
Inputs may be any that keep to these rules, and one draw needn't show every extreme that they name: `order`: each position once. `segment`: never falls along positions; every document 1 to 2048 positions long.
All inputs are finite; a program needn't handle non-finite values.
Results may differ from a plain program's by a relative error of at most 0.03.
Values may be sent and summed in bfloat16 or wider, within the bound.
A program may use at most 64 MiB of HBM per device.

v0:
```python
import math

import jax
import jax.numpy as jnp
from jax import lax
from jax.sharding import PartitionSpec as P

HD = 128


NEG = -1e30


def masked_scores(query_four, key_block, scale, mask):
    scores = (
        jnp.einsum("qgrd,kgd->qgrk", query_four, key_block, preferred_element_type=jnp.float32)
        * scale
    )
    return jnp.where(mask[:, None, None, :], scores, NEG)


def grad_terms(query_four, grad_four, log_total, delta, key_block, value_block, mask, scale):
    scores = masked_scores(query_four, key_block, scale, mask)
    probs = jnp.where(mask[:, None, None, :], jnp.exp(scores - log_total[..., None]), 0.0)
    grad_probs = jnp.einsum(
        "qgrd,kgd->qgrk", grad_four, value_block, preferred_element_type=jnp.float32
    )
    grad_scores = (probs * (grad_probs - delta[..., None]) * scale).astype(jnp.bfloat16)
    return (probs.astype(jnp.bfloat16), grad_scores)


def per_device(query, key_proj, value, out_weight, grad_out, order, segment):
    rows = query.shape[0]
    count = lax.axis_size("context")
    place = lax.axis_index("context")
    heads = query.shape[1] // HD
    groups = key_proj.shape[1] // HD
    ratio = heads // groups
    tokens = rows * count
    scale = 1.0 / math.sqrt(HD)
    block = math.gcd(tokens, 512)
    blocks = tokens // block
    own_order = lax.dynamic_slice_in_dim(order, place * rows, rows)
    own_segment = jnp.take(segment, own_order)
    row_segment = jnp.take(segment, order)
    query_four = query.reshape(rows, groups, ratio, HD)
    keys_all, values_all = (
        lax.all_gather(key_proj, "context", axis=0, tiled=True),
        lax.all_gather(value, "context", axis=0, tiled=True),
    )
    key_blocks = keys_all.reshape(blocks, block, groups, HD)
    value_blocks = values_all.reshape(blocks, block, groups, HD)
    order_blocks = order.reshape(blocks, block)
    segment_blocks = row_segment.reshape(blocks, block)

    def block_mask(order_block, segment_block):
        return (own_segment[:, None] == segment_block[None, :]) & (
            order_block[None, :] <= own_order[:, None]
        )

    def stats_step(carry, inputs):
        top, total = carry
        key_block, order_block, segment_block = inputs
        scores = masked_scores(query_four, key_block, scale, block_mask(order_block, segment_block))
        new_top = jnp.maximum(top, jnp.max(scores, axis=-1))
        total = total * jnp.exp(top - new_top) + jnp.sum(
            jnp.exp(scores - new_top[..., None]), axis=-1
        )
        return ((new_top, total), None)

    start_top = jnp.full((rows, groups, ratio), NEG, jnp.float32)
    (top, total), _ = lax.scan(
        stats_step,
        (start_top, jnp.zeros_like(start_top)),
        (key_blocks, order_blocks, segment_blocks),
    )
    log_total = top + jnp.log(total)

    def output_step(accum, inputs):
        key_block, value_block, order_block, segment_block = inputs
        mask = block_mask(order_block, segment_block)
        scores = masked_scores(query_four, key_block, scale, mask)
        probs = jnp.where(
            mask[:, None, None, :], jnp.exp(scores - log_total[..., None]), 0.0
        ).astype(jnp.bfloat16)
        accum = accum + jnp.einsum(
            "qgrk,kgd->qgrd", probs, value_block, preferred_element_type=jnp.float32
        )
        return (accum, None)

    empty_rows = jnp.zeros((rows, groups, ratio, HD), jnp.float32)
    accum, _ = lax.scan(
        output_step, empty_rows, (key_blocks, value_blocks, order_blocks, segment_blocks)
    )
    attended_four = accum.astype(jnp.bfloat16)
    attended = attended_four.reshape(rows, heads * HD)
    partial_value = jnp.dot(attended, out_weight, preferred_element_type=jnp.float32)
    output = lax.psum_scatter(partial_value, "tensor", scatter_dimension=1, tiled=True).astype(
        jnp.bfloat16
    )
    grad_sum = lax.dot_general(
        lax.all_gather(grad_out, "tensor", axis=1, tiled=True),
        out_weight,
        (((1,), (1,)), ((), ())),
        preferred_element_type=jnp.float32,
    )
    grad_attended = grad_sum.astype(jnp.bfloat16)
    grad_four = grad_attended.reshape(rows, groups, ratio, HD)
    delta = jnp.sum(grad_four.astype(jnp.float32) * attended_four.astype(jnp.float32), axis=-1)

    def grad_step(carry, inputs):
        key_block, value_block, order_block, segment_block = inputs
        mask = block_mask(order_block, segment_block)
        probs, grad_scores = grad_terms(
            query_four, grad_four, log_total, delta, key_block, value_block, mask, scale
        )
        carry = carry + jnp.einsum(
            "qgrk,kgd->qgrd", grad_scores, key_block, preferred_element_type=jnp.float32
        )
        key_part = jnp.einsum(
            "qgrk,qgrd->kgd", grad_scores, query_four, preferred_element_type=jnp.float32
        )
        value_part = jnp.einsum(
            "qgrk,qgrd->kgd", probs, grad_four, preferred_element_type=jnp.float32
        )
        return (carry, (key_part, value_part))

    query_sum, (key_parts, value_parts) = lax.scan(
        grad_step, empty_rows, (key_blocks, value_blocks, order_blocks, segment_blocks)
    )
    key_parts = key_parts.reshape(count, rows, groups * HD)
    value_parts = value_parts.reshape(count, rows, groups * HD)
    key_in, value_in = (
        lax.all_to_all(key_parts, "context", split_axis=0, concat_axis=0, tiled=True),
        lax.all_to_all(value_parts, "context", split_axis=0, concat_axis=0, tiled=True),
    )
    grad_key = jnp.sum(key_in, axis=0).astype(jnp.bfloat16)
    grad_value = jnp.sum(value_in, axis=0).astype(jnp.bfloat16)
    grad_query = query_sum.astype(jnp.bfloat16).reshape(rows, heads * HD)
    return (output, grad_query, grad_key, grad_value)


def solution(mesh):
    return jax.shard_map(
        per_device,
        mesh=mesh,
        in_specs=(
            P("context", "tensor"),
            P("context", "tensor"),
            P("context", "tensor"),
            P("tensor", None),
            P("context", "tensor"),
            P(),
            P(),
        ),
        out_specs=(
            P("context", "tensor"),
            P("context", "tensor"),
            P("context", "tensor"),
            P("context", "tensor"),
        ),
        check_vma=False,
    )
```

profile of v0, /device:TPU:24, one launch (start us, length us, event | category | flops | bytes accessed | tf_op | source)
XLA Modules:
  0.0 832.0 jit_solution(18134568498793507356)
XLA Ops:
  12.9 1.7 gather_fusion
  14.6 45.5 %gather_fusion.1 = s32[8192]{0:T(1024)S(1)} fusion(s32[8192]{0:T(1024)S(1)} %copy-done.1, s32[8192]{0:T(1024)S(1)} %fusion.61), kind=kCustom, calls=%fused_computation.1 | custom fusion | bytes 98304 | tf_op jit(solution)/shard_map/jit(_take)/gather | solution.py:45
  60.2 2.1 convolution_convert_fusion
  62.4 126.8 %all-gather.6.cloned.1.call-done = bf16[8192,128]{1,0:T(8,128)(2,1)} async-done(((bf16[128,128]{1,0:T(8,128)(2,1)}), bf16[8192,128]{1,0:T(8,128)(2,1)}) %all-gather.6.cloned.1.call-update) | async-done | bytes 2097168 | tf_op jit(solution)/shard_map/all_gather | solution.py:48
  189.3 24.9 %while.39 = (s32[]{:T(128)}, f32[128,1,2]{0,2,1:T(2,128)S(1)}, f32[128,1,2]{0,2,1:T(2,128)S(1)}, s32[128]{0:T(128)S(1)}, s32[16,512]{1,0:T(8,128)S(1)}, /*index=...) while((s32[]{:T(128)}, f32[128,1,2]{0,2,1:T(2,128)S(1)}, ...), condition=%wide.region_3.4_spmd.clone, body=%wide.region_0.3_spmd.clone.sunk | while | flops 34407680 | bytes 1403516 | solution.py:72
  214.2 115.0 %all-gather.4.cloned.1.call-done = bf16[8192,128]{1,0:T(8,128)(2,1)} async-done(((bf16[128,128]{1,0:T(8,128)(2,1)}), bf16[8192,128]{1,0:T(8,128)(2,1)}) %all-gather.4.cloned.1.call-update) | async-done | bytes 2097168 | tf_op jit(solution)/shard_map/all_gather | solution.py:49
  329.2 27.2 %while.40 = (s32[]{:T(128)}, f32[128,1,2,128]{0,3,2,1:T(8,128)S(1)}, bf16[16,512,1,128]{3,1,2,0:T(8,128)(2,1)}, s32[128]{0:T(128)S(1)}, s32[16,512]{1,0:T(8,128)...) while((s32[]{:T(128)}, ...), condition=%wide.region_5.6_spmd.clone, body=%wide.region_4.5_spmd.clone.sunk | while | flops 68026368 | bytes 736387 | solution.py:92
  332.8 1.4 fusion.94
  334.5 1.4 fusion.94
  337.9 1.4 fusion.94
  341.3 1.4 fusion.94
  343.0 1.4 fusion.94
  346.4 1.4 fusion.94
  349.8 1.4 fusion.94
  351.5 1.4 fusion.94
  356.4 90.1 %while.41 = (s32[]{:T(128)}, f32[128,1,2,128]{0,3,2,1:T(8,128)S(1)}, f32[16,512,1,128]{3,1,2,0:T(8,128)}, f32[16,512,1,128]{3,1,2,0:T(8,128)}, bf16[16,512,1,128...) while((s32[]{:T(128)}, ...), condition=%wide.region_9.10_spmd.clone, body=%wide.region_8.9_spmd.clone.sunk | while | flops 169213952 | bytes 3950243 | solution.py:128
  446.6 187.1 %all_to_all.10 = f32[64,128,128]{2,1,0:T(8,128)} all-to-all(f32[64,128,128]{2,1,0:T(8,128)} %bitcast.258), channel_id=1, replica_groups=mesh['context'=64,'tensor'=8] {'context'}, dimensions={0} | all-to-all | bytes 8388608 | tf_op jit(solution)/shard_map/all_to_all | solution.py:134
  633.7 9.0 %all-to-all-start.1 = ((f32[64,128,128]{2,1,0:T(8,128)}), f32[64,128,128]{2,1,0:T(8,128)}, u32[]{:S(2)}, u32[]{:S(2)}) async-start(f32[64,128,128]{2,1,0:T(8,128)} %bitcast.259), calls=%async_computation.2 | async-start | bytes 8388608 | tf_op jit(solution)/shard_map/all_to_all | solution.py:135
  642.7 1.8 fusion.63
  645.3 40.4 %reduce-scatter.2.cloned.1.call-done = f32[128,512]{1,0:T(8,128)} async-done(((f32[128,4096]{1,0:T(8,128)}), f32[128,512]{1,0:T(8,128)}) %reduce-scatter.2.cloned.1.call-update) | async-done | bytes 262160 | tf_op jit(solution)/shard_map/reduce_scatter | solution.py:98
  685.6 1.6 convert_element_type.42
  687.3 3.0 reduce_sum.42
  690.3 132.2 %all-to-all-done.1 = f32[64,128,128]{2,1,0:T(8,128)} async-done(((f32[64,128,128]{2,1,0:T(8,128)}), f32[64,128,128]{2,1,0:T(8,128)}, u32[]{:S(2)}, u32[]{:S(2)}) %all-to-all-start.1) | async-done | bytes 4194336 | tf_op jit(solution)/shard_map/all_to_all | solution.py:135
  822.5 3.0 reduce_sum.43
  (301 shorter events, 134.9 us)
Async XLA Ops:
  7.2 53.0 %copy-start = (bf16[256,4096]{1,0:T(8,128)(2,1)S(1)}, bf16[256,4096]{1,0:T(8,128)(2,1)}, u32[]{:S(2)}) copy-start(bf16[256,4096]{1,0:T(8,128)(2,1)} %param.16) | copy-start | bytes 6291460
  7.2 7.4 copy-start.1
  7.2 53.0 %all-gather.8.cloned.1.call-start = ((), (), s32[]{:S(2)}) async-start(), calls=%async_computation.6 | async-start | bytes 1179648 | tf_op jit(solution)/shard_map/all_gather | solution.py:102
  7.9 181.3 %all-gather.6.cloned.1.call-start = ((), (), s32[]{:S(2)}) async-start(), calls=%async_computation.4 | async-start | bytes 2129920 | tf_op jit(solution)/shard_map/all_gather | solution.py:48
  8.7 320.5 %all-gather.4.cloned.1.call-start = ((), (), s32[]{:S(2)}) async-start(), calls=%async_computation.3 | async-start | bytes 2129920 | tf_op jit(solution)/shard_map/all_gather | solution.py:49
  14.6 45.5 %copy-start.2 = (s32[8192]{0:T(1024)S(1)}, s32[8192]{0:T(1024)}, u32[]{:S(2)}) copy-start(s32[8192]{0:T(1024)} %param.18) | copy-start | bytes 98308
  633.7 188.8 %all-to-all-start.1 = ((f32[64,128,128]{2,1,0:T(8,128)}), f32[64,128,128]{2,1,0:T(8,128)}, u32[]{:S(2)}, u32[]{:S(2)}) async-start(f32[64,128,128]{2,1,0:T(8,128)} %bitcast.259), calls=%async_computation.2 | async-start | bytes 8388608 | tf_op jit(solution)/shard_map/all_to_all | solution.py:135
  642.6 43.0 %reduce-scatter.2.cloned.1.call-start = ((), (), s32[]{:S(2)}) async-start(), calls=%async_computation.5 | async-start | bytes 2359296 | tf_op jit(solution)/shard_map/reduce_scatter | solution.py:98
Sparse Core Ops, SparseCore 0:
  10.2 33.9 all-gather.7
  47.1 142.1 all-gather.5
  192.2 136.9 all-gather.3
  646.0 39.5 reduce-scatter.1
where the time goes:
time: 834 us; the launch traced here: 832 us
  waiting for transfers between devices  417 us (50%)
  blocking collectives  187 us (22%)
  matrix products  132 us (16%)
  local copies, waits for them, and re-layouts  50.6 us (6%)
  other arithmetic  20.9 us (3%)
  between operations  14 us (2%)
  starting transfers between devices  9.11 us (1%)
    all_to_all x1, blocking collectives, per_device(): lax.all_to_all(key_parts, 'context', split_axis=0, concat_axis=0, tiled=T...  187 us
    all_to_all x1, waiting for transfers between devices, per_device(): lax.all_to_all(value_parts, 'context', split_axis=0, concat_axis=0, tiled...  132 us
    all_gather x1, waiting for transfers between devices, per_device(): lax.all_gather(key_proj, 'context', axis=0, tiled=True)  127 us
    all_gather x1, waiting for transfers between devices, per_device(): lax.all_gather(value, 'context', axis=0, tiled=True)  115 us
    gather x1, local copies, waits for them, and re-layouts, per_device(): row_segment = jnp.take(segment, order)  45.5 us
    reduce_scatter x1, waiting for transfers between devices, per_device(): lax.psum_scatter(partial_value, 'tensor', scatter_dimension=1, tiled=True)  40.4 us
    dot_general x32, matrix products, masked_scores(): jnp.einsum('qgrd,kgd->qgrk', query_four, key_block, preferred_element_typ...  37.7 us
    dot_general x16, matrix products, output_step(): jnp.einsum('qgrk,kgd->qgrd', probs, value_block, preferred_element_type=j...  23.1 us
  transfers between devices with their start and end apart: 5, of which 4 were waited for; matrix products, arithmetic and copies ran while one was open for 10% of the time, Pallas kernels for 0%

commit v1 on v0

v1 whole, which is shorter than its diff:
```python
import functools
import math

import jax
import jax.numpy as jnp
from jax import lax
from jax.experimental import pallas as pl
from jax.experimental.pallas import tpu as pltpu
from jax.sharding import PartitionSpec as P

MESH = pl.DeviceIdType.MESH
NEG = -1e30
HD = 128
ROWS = 128
HEADS = 2
BF = jnp.bfloat16
F32 = jnp.float32
FACTORS = {64: (4, 16)}

NN = (((1,), (0,)), ((), ()))
NT = (((1,), (1,)), ((), ()))
TN = (((0,), (0,)), ((), ()))


def mm(a, b, dims):
    return lax.dot_general(a, b, dims, preferred_element_type=F32)


def at128(index):
    return pl.ds(pl.multiple_of(index * 128, 128), 128)


def at256(index):
    return pl.ds(pl.multiple_of(index * 256, 256), 256)


def kernel(
    nx, nz, ny, docs,
    q_hbm, k_hbm, v_hbm, w_hbm, g_hbm, order_hbm, segment_hbm,
    out_hbm, dq_hbm, dk_hbm, dv_hbm,
    q_own, w, order, segment, kbuf, vbuf, q_t, do_t, g_all,
    pos_row, pos_key, scores, probs, dscores, top, total, o_t, dq_t,
    stats, o_send, o_recv, factor, delta, fdo_t, fq_t,
    dk_part, dv_part, rs_send, rs_recv, dq_send, dq_recv,
    part_own, part_send, part_recv, y_send, y_recv,
    out_v, dq_v, dk_v, dv_v,
    in_sem, out_sem, kv_s, kv_r, q_s, q_r, do_s, do_r, st_s, st_r, o_s, o_r, dq_s, dq_r,
    gy_s, gy_r, gc_s, gc_r, pc_s, pc_r, py_s, py_r, rs_s, rs_r,
):
    context, tensor = lax.axis_index("context"), lax.axis_index("tensor")
    x, z = context // nz, lax.rem(context, nz)
    y, core = tensor // 2, lax.rem(tensor, 2)
    half = nz // 2
    exponent = math.log2(math.e) / math.sqrt(HD)
    scale = 1.0 / math.sqrt(HD)
    right = (x * nz + lax.rem(z + 1, nz), tensor)
    left = (x * nz + lax.rem(z + nz - 1, nz), tensor)
    x_at = [lax.rem(x + d, nx) for d in range(nx)]
    x_peer = [(x_at[d] * nz + z, tensor) for d in range(nx)]
    y_at = [lax.rem(y + d, ny) for d in range(ny)]
    y_peer = [(context, y_at[d] * 2 + core) for d in range(ny)]
    partner = (context, y * 2 + 1 - core)

    def remote(src, dst, send, recv, device):
        return pltpu.make_async_remote_copy(
            src_ref=src, dst_ref=dst, send_sem=send, recv_sem=recv, device_id=device, device_id_type=MESH
        )

    load_q = pltpu.make_async_copy(q_hbm, q_own, in_sem.at[0])
    load_order = pltpu.make_async_copy(order_hbm, order, in_sem.at[1])
    load_segment = pltpu.make_async_copy(segment_hbm, segment, in_sem.at[2])
    load_k = pltpu.make_async_copy(k_hbm, kbuf.at[at128(z)], in_sem.at[3])
    load_v = pltpu.make_async_copy(v_hbm, vbuf.at[at128(z)], in_sem.at[4])
    load_g = pltpu.make_async_copy(g_hbm, g_all.at[tensor], in_sem.at[5])
    load_w = pltpu.make_async_copy(w_hbm, w, in_sem.at[6])
    for load in (load_q, load_order, load_segment, load_k, load_v, load_g, load_w):
        load.start()

    barrier = pltpu.get_barrier_semaphore()
    peers = [right, left] + x_peer[1:] + y_peer[1:] + [partner]
    for peer in peers:
        pl.semaphore_signal(barrier, inc=1, device_id=peer, device_id_type=MESH)

    load_q.wait()
    for h in range(HEADS):
        q_t[:, at128(x * HEADS + h)] = q_own[:, h * HD : (h + 1) * HD].T

    pl.semaphore_wait(barrier, len(peers))

    def kv_copy(stream, step):
        buf = kbuf if stream < 2 else vbuf
        hop = step if stream % 2 == 0 else -step
        slot = buf.at[at128(lax.rem(z - hop + 2 * nz, nz))]
        return remote(slot, slot, kv_s.at[stream, step], kv_r.at[stream, step], right if stream % 2 == 0 else left)

    def kv_first(stream):
        src, buf = (k_hbm, kbuf) if stream < 2 else (v_hbm, vbuf)
        return remote(src, buf.at[at128(z)], kv_s.at[stream, 0], kv_r.at[stream, 0], right if stream % 2 == 0 else left)

    kv_steps = (half, half - 1, half - 1, half)

    def q_copy(d):
        slot = q_t.at[:, at256(x)]
        return remote(slot, slot, q_s.at[d], q_r.at[d], x_peer[d])

    def do_copy(d):
        slot = do_t.at[:, at256(x)]
        return remote(slot, slot, do_s.at[d], do_r.at[d], x_peer[d])

    def gy_copy(d):
        return remote(g_hbm, g_all.at[tensor], gy_s.at[d], gy_r.at[d], y_peer[d])

    def gc_copy(d):
        at = y_at[d] * 2 + core
        return remote(g_hbm if d == 0 else g_all.at[at], g_all.at[at], gc_s.at[d], gc_r.at[d], partner)

    for stream in (0, 1):
        if kv_steps[stream]:
            kv_first(stream).start()
    for d in range(1, nx):
        q_copy(d).start()
    for stream in (2, 3):
        if kv_steps[stream]:
            kv_first(stream).start()
    for d in range(1, ny):
        gy_copy(d).start()
    gc_copy(0).start()

    load_order.wait()
    load_segment.wait()
    starts = [
        jnp.sum(jnp.where(segment[...] < d, 1, 0), axis=(0, 1), keepdims=True) for d in range(1, docs)
    ]
    for xp in range(nx):
        own = order[pl.ds(xp * nz + z, 1), :]
        first = jnp.zeros_like(own)
        for start in starts:
            first = jnp.maximum(first, jnp.where(start <= own, start, 0))
        pos_row[xp : xp + 1, :] = own
        pos_row[nx + xp : nx + xp + 1, :] = first

    @pl.loop(0, nz)
    def _(b):
        row = order[pl.ds(x * nz + b, 1), :]
        pos_key[at128(b), :] = jnp.broadcast_to(row, (ROWS, 128)).T

    top[...] = jnp.full_like(top, NEG)
    load_k.wait()
    for d in range(1, nx):
        q_copy(d).wait_recv()

    def score_block(b):
        raw = mm(kbuf[at128(b), :], q_t[...], NN)
        key = pos_key[at128(b), :]
        for xp in range(nx):
            mask = (key >= pos_row[nx + xp : nx + xp + 1, :]) & (key <= pos_row[xp : xp + 1, :])
            for h in range(HEADS):
                lanes = slice((xp * HEADS + h) * 128, (xp * HEADS + h + 1) * 128)
                part = jnp.where(mask, raw[:, lanes], NEG)
                scores[at128(b), lanes] = part
                top[:, lanes] = jnp.maximum(top[:, lanes], jnp.max(part.reshape(ROWS // 8, 8, 128), axis=0))

    score_block(z)

    def cotangent():
        load_w.wait()
        load_g.wait()
        for d in range(ny):
            gc_copy(d).wait_recv()
        acc = jnp.zeros((HEADS * HD, ROWS), F32)
        features = g_hbm.shape[1]
        for t in range(2 * ny):
            acc = acc + mm(w[:, t * features : (t + 1) * features], g_all[t], NT)
        for h in range(HEADS):
            do_t[:, at128(x * HEADS + h)] = acc[h * HD : (h + 1) * HD, :].astype(BF)
        for d in range(1, nx):
            do_copy(d).start()

    def cotangent_relay():
        for d in range(1, ny):
            gy_copy(d).wait_recv()
        for d in range(1, ny):
            gc_copy(d).start()

    relay_at, cotangent_at = min(3, half - 1), min(4, half - 1)

    @pl.loop(0, half)
    def _(step):
        def arrive(stream):
            @pl.when(step < kv_steps[stream])
            def _():
                kv_copy(stream, step).wait_recv()

            @pl.when(step + 1 < kv_steps[stream])
            def _():
                kv_copy(stream, step + 1).start()

        arrive(0)
        arrive(1)
        score_block(lax.rem(z - 1 - step + nz, nz))
        arrive(2)
        arrive(3)

        @pl.when(step < half - 1)
        def _():
            score_block(lax.rem(z + 1 + step, nz))

        @pl.when(step == relay_at)
        def _():
            cotangent_relay()

        @pl.when(step == cotangent_at)
        def _():
            cotangent()

    load_v.wait()
    peak = jnp.max(top[...], axis=0, keepdims=True)
    total[...] = jnp.zeros_like(total)
    o_t[...] = jnp.zeros_like(o_t)
    keys = nz * ROWS
    chunk = min(512, keys)
    width = nx * HEADS * 128

    @pl.loop(0, keys // 128)
    def _(i):
        p = jnp.exp2((scores[at128(i), :] - peak) * exponent)
        probs[at128(i), :] = p.astype(BF)
        total[...] += jnp.sum(p.reshape(16, 8, width), axis=0)

    @pl.loop(0, keys // chunk)
    def _(i):
        at = pl.ds(pl.multiple_of(i * chunk, chunk), chunk)
        o_t[...] += mm(vbuf[at, :], probs[at, :], TN)

    for d in range(1, nx):
        do_copy(d).wait_recv()
    sums = jnp.sum(total[...], axis=0, keepdims=True)
    inner = jnp.sum(o_t[...] * do_t[...].astype(F32), axis=0, keepdims=True)
    slots = nx * HEADS
    for s in range(slots):
        lanes = slice(s * 128, (s + 1) * 128)
        stats[x, 0, s : s + 1, :] = peak[:, lanes]
        stats[x, 1, s : s + 1, :] = sums[:, lanes]
        stats[x, 2, s : s + 1, :] = inner[:, lanes]
    o_send[...] = o_t[...].astype(BF)

    def st_copy(d):
        return remote(stats.at[x], stats.at[x], st_s.at[d], st_r.at[d], x_peer[d])

    def o_copy(d):
        return remote(o_send.at[:, at256(x_at[d])], o_recv.at[d], o_s.at[d], o_r.at[d], x_peer[d])

    for d in range(1, nx):
        st_copy(d).start()
    for d in range(1, nx):
        o_copy(d).start()
    for d in range(1, nx):
        st_copy(d).wait_recv()

    peak_all = functools.reduce(jnp.maximum, [stats[i, 0] for i in range(nx)])
    weight = [jnp.exp2((stats[i, 0] - peak_all) * exponent) for i in range(nx)]
    inverse = 1.0 / functools.reduce(jnp.add, [weight[i] * stats[i, 1] for i in range(nx)])
    delta[...] = inverse * functools.reduce(jnp.add, [weight[i] * stats[i, 2] for i in range(nx)])
    for i in range(nx):
        factor[i] = weight[i] * inverse
    mine = factor[x]
    for s in range(slots):
        lanes = slice(s * 128, (s + 1) * 128)
        f = mine[s : s + 1, :]
        fdo_t[:, lanes] = (do_t[:, lanes].astype(F32) * f).astype(BF)
        fq_t[:, lanes] = (q_t[:, lanes].astype(F32) * (f * scale)).astype(BF)

    dq_t[...] = jnp.zeros_like(dq_t)

    def grad_block(b):
        p = probs[at128(b), :]
        dp = mm(vbuf[at128(b), :], do_t[...], NN)
        for s in range(slots):
            lanes = slice(s * 128, (s + 1) * 128)
            dscores[at128(b), lanes] = (p[:, lanes].astype(F32) * (dp[:, lanes] - delta[s : s + 1, :])).astype(BF)
        ds = dscores[at128(b), :]
        dv_part[b] = mm(p, fdo_t[...], NT)
        dk_part[b] = mm(ds, fq_t[...], NT)
        dq_t[...] += mm(kbuf[at128(b), :], ds, TN)

    def rs_copy(stream, step):
        return remote(
            rs_send.at[stream, step], rs_recv.at[stream, step], rs_s.at[stream, step], rs_r.at[stream, step],
            right if stream % 2 == 0 else left,
        )

    rs_from = (0, 1, 1, 0)

    def rs_step(stream, step):
        hop = half - step
        owner = lax.rem(z + (hop if stream % 2 == 0 else nz - hop), nz)
        part = dk_part if stream < 2 else dv_part

        @pl.when(step == rs_from[stream])
        def _():
            rs_send[stream, step] = part[owner].astype(BF)
            rs_copy(stream, step).start()

        @pl.when(step > rs_from[stream])
        def _():
            rs_copy(stream, step - 1).wait_recv()
            rs_send[stream, step] = (part[owner] + rs_recv[stream, step - 1].astype(F32)).astype(BF)
            rs_copy(stream, step).start()

    def dq_copy(d):
        return remote(dq_send.at[:, at256(x_at[d])], dq_recv.at[d], dq_s.at[d], dq_r.at[d], x_peer[d])

    def pc_copy():
        return remote(part_send, part_recv, pc_s.at[0], pc_r.at[0], partner)

    def py_copy(d):
        return remote(y_send.at[y_at[d]], y_recv.at[d], py_s.at[d], py_r.at[d], y_peer[d])

    features = g_hbm.shape[1]

    def project():
        for d in range(1, nx):
            o_copy(d).wait_recv()
        attended = []
        for h in range(HEADS):
            acc = o_send[:, at128(x * HEADS + h)].astype(F32) * factor[x, pl.ds(x * HEADS + h, 1), :]
            for d in range(1, nx):
                source = lax.rem(x - d + nx, nx)
                acc = acc + (
                    o_recv[d, :, h * 128 : (h + 1) * 128].astype(F32) * factor[source, pl.ds(x * HEADS + h, 1), :]
                )
            attended.append(acc.astype(BF))
        attended = jnp.concatenate(attended, axis=0)

        @pl.loop(0, ny)
        def _(yp):
            for c in range(2):
                at = pl.ds(pl.multiple_of((yp * 2 + c) * features, features), features)
                part = mm(attended, w[:, at], TN)

                @pl.when(core == c)
                def _():
                    part_own[yp] = part

                @pl.when(core != c)
                def _():
                    part_send[yp] = part.astype(BF)

        pc_copy().start()

    def spread():
        pc_copy().wait_recv()

        @pl.loop(0, ny)
        def _(yp):
            part = part_own[yp] + part_recv[yp].astype(F32)
            part_own[yp] = part
            y_send[yp] = part.astype(BF)

        for d in range(1, ny):
            py_copy(d).start()

    def send_dq():
        for s in range(slots):
            lanes = slice(s * 128, (s + 1) * 128)
            dq_t[:, lanes] = dq_t[:, lanes] * (factor[x, s : s + 1, :] * scale)
        dq_send[...] = dq_t[...].astype(BF)
        for d in range(1, nx):
            dq_copy(d).start()

    ahead = half // 2
    project_at, spread_at = min(1, half - 1), min(3, half - 1)
    grad_block(lax.rem(z + half, nz))

    @pl.loop(0, half)
    def _(step):
        for stream in (3, 0, 1, 2):
            rs_step(stream, step)

        @pl.when(step < max(1, ahead))
        def _():
            for later in range(2 if ahead else 1):
                hop = half - ((2 if ahead else 1) * step + 1 + later)
                grad_block(lax.rem(z + hop + nz, nz))

                @pl.when(hop > 0)
                def _():
                    grad_block(lax.rem(z - hop + nz, nz))

        @pl.when(step == max(1, ahead) - 1)
        def _():
            send_dq()

        @pl.when(step == project_at)
        def _():
            project()

        @pl.when(step == spread_at)
        def _():
            spread()

    for d in range(1, ny):
        py_copy(d).wait_recv()
    out = part_own[y]
    for d in range(1, ny):
        out = out + y_recv[d].astype(F32)
    out_v[...] = out.astype(BF)
    store_out = pltpu.make_async_copy(out_v, out_hbm, out_sem.at[0])
    store_out.start()

    for d in range(1, nx):
        dq_copy(d).wait_recv()
    for h in range(HEADS):
        acc = dq_t[:, at128(x * HEADS + h)]
        for d in range(1, nx):
            acc = acc + dq_recv[d, :, h * 128 : (h + 1) * 128].astype(F32)
        dq_v[:, h * 128 : (h + 1) * 128] = acc.T.astype(BF)
    store_dq = pltpu.make_async_copy(dq_v, dq_hbm, out_sem.at[1])
    store_dq.start()

    def owned(part, streams):
        acc = part[z]
        for stream in streams:
            if half > rs_from[stream]:
                rs_copy(stream, half - 1).wait_recv()
                acc = acc + rs_recv[stream, half - 1].astype(F32)
        return acc.astype(BF)

    dv_v[...] = owned(dv_part, (2, 3))
    store_dv = pltpu.make_async_copy(dv_v, dv_hbm, out_sem.at[2])
    store_dv.start()
    dk_v[...] = owned(dk_part, (0, 1))
    store_dk = pltpu.make_async_copy(dk_v, dk_hbm, out_sem.at[3])
    store_dk.start()

    for stream in range(4):
        for step in range(half):
            if step < kv_steps[stream]:
                (kv_first(stream) if step == 0 else kv_copy(stream, step)).wait_send()
            if step >= rs_from[stream]:
                rs_copy(stream, step).wait_send()
    for d in range(1, nx):
        for copy in (q_copy, do_copy, st_copy, o_copy, dq_copy):
            copy(d).wait_send()
    for d in range(1, ny):
        gy_copy(d).wait_send()
        py_copy(d).wait_send()
    for d in range(ny):
        gc_copy(d).wait_send()
    pc_copy().wait_send()
    for store in (store_out, store_dq, store_dv, store_dk):
        store.wait()


def per_device(nx, nz, ny, docs, query, key_proj, value, out_weight, grad_out, order, segment):
    features = grad_out.shape[1]
    half = nz // 2
    keys, width, slots = nz * ROWS, nx * HEADS * 128, nx * HEADS
    tokens = order.shape[0]
    order = order.reshape(tokens // 128, 128)
    segment = segment.reshape(tokens // 128, 128)

    def vm(*shape, dtype=BF):
        return pltpu.VMEM(shape, dtype)

    def sem(*shape):
        return pltpu.SemaphoreType.DMA(shape)

    scratch = [
        vm(ROWS, HEADS * HD), vm(HEADS * HD, out_weight.shape[1]),
        vm(tokens // 128, 128, dtype=jnp.int32), vm(tokens // 128, 128, dtype=jnp.int32),
        vm(keys, HD), vm(keys, HD), vm(HD, width), vm(HD, width), vm(2 * ny, ROWS, features),
        vm(2 * nx, 128, dtype=jnp.int32), vm(keys, 128, dtype=jnp.int32),
        vm(keys, width, dtype=F32), vm(keys, width), vm(keys, width),
        vm(8, width, dtype=F32), vm(8, width, dtype=F32), vm(HD, width, dtype=F32), vm(HD, width, dtype=F32),
        vm(nx, 3, slots, 128, dtype=F32), vm(HD, width), vm(nx, HD, 256),
        vm(nx, slots, 128, dtype=F32), vm(slots, 128, dtype=F32), vm(HD, width), vm(HD, width),
        vm(nz, ROWS, HD, dtype=F32), vm(nz, ROWS, HD, dtype=F32),
        vm(4, half, ROWS, HD), vm(4, half, ROWS, HD), vm(HD, width), vm(nx, HD, 256),
        vm(ny, ROWS, features, dtype=F32), vm(ny, ROWS, features), vm(ny, ROWS, features),
        vm(ny, ROWS, features), vm(ny, ROWS, features),
        vm(ROWS, features), vm(ROWS, HEADS * HD), vm(ROWS, HD), vm(ROWS, HD),
        sem(7), sem(4), sem(4, half), sem(4, half),
    ] + [sem(nx)] * 10 + [sem(ny)] * 4 + [sem(1)] * 2 + [sem(ny)] * 2 + [sem(4, half)] * 2
    flops = 2 * width * keys * HD * 6 + 4 * ROWS * HEADS * HD * out_weight.shape[1]
    return pl.pallas_call(
        functools.partial(kernel, nx, nz, ny, docs),
        out_shape=[
            jax.ShapeDtypeStruct((ROWS, features), BF),
            jax.ShapeDtypeStruct((ROWS, HEADS * HD), BF),
            jax.ShapeDtypeStruct((ROWS, HD), BF),
            jax.ShapeDtypeStruct((ROWS, HD), BF),
        ],
        in_specs=[pl.BlockSpec(memory_space=pl.ANY)] * 7,
        out_specs=[pl.BlockSpec(memory_space=pl.ANY)] * 4,
        scratch_shapes=scratch,
        compiler_params=pltpu.CompilerParams(
            collective_id=0, has_side_effects=True, vmem_limit_bytes=48 * 1024 * 1024
        ),
        cost_estimate=pl.CostEstimate(flops=flops, bytes_accessed=4 << 20, transcendentals=keys * width),
    )(query, key_proj, value, out_weight, grad_out, order, segment)


def solution(mesh):
    nx, nz = FACTORS[mesh.shape["context"]]
    ny = mesh.shape["tensor"] // 2
    return jax.shard_map(
        functools.partial(per_device, nx, nz, ny, 8),
        mesh=mesh,
        in_specs=(
            P("context", "tensor"),
            P("context", "tensor"),
            P("context", "tensor"),
            P("tensor", None),
            P("context", "tensor"),
            P(),
            P(),
        ),
        out_specs=(P("context", "tensor"),) * 4,
        check_vma=False,
    )
```

time: 834 us -> 89 us (0.11)
  waiting for transfers between devices: 417 us -> 0 us
  blocking collectives: 187 us -> 0 us
  matrix products: 132 us -> 0 us
  Pallas kernels: 0 us -> 78.8 us
  local copies, waits for them, and re-layouts: 50.6 us -> 8.87 us
  other arithmetic: 20.9 us -> 0 us
  between operations: 14 us -> 0.66 us
  starting transfers between devices: 9.11 us -> 0 us
    all_gather x3 -> x0, waiting for transfers between devices: 242 us -> none  [the longest x1 127 us: per_device(): lax.all_gather(key_proj, 'context', axis=0, tiled=True)]
    all_to_all x1 -> x0, blocking collectives: 187 us -> none  [per_device(): lax.all_to_all(key_parts, 'context', split_axis=0, concat_axis=0, tiled=T...]
    all_to_all x1 -> x0, waiting for transfers between devices: 132 us -> none  [per_device(): lax.all_to_all(value_parts, 'context', split_axis=0, concat_axis=0, tiled...]
    dot_general x114 -> x0, matrix products: 132 us -> none  [the longest x32 37.7 us: masked_scores(): jnp.einsum('qgrd,kgd->qgrk', query_four, key_block, preferred_element_typ...]
    pallas_call x0 -> x1, Pallas kernels: none -> 78.8 us  [per_device(): pl.pallas_call(functools.partial(kernel, nx, nz, ny, docs), out_shape=[ja...]
    gather x2 -> x0, local copies, waits for them, and re-layouts: 47.2 us -> none  [the longest x1 45.5 us: per_device(): row_segment = jnp.take(segment, order)]
    reduce_scatter x1 -> x0, waiting for transfers between devices: 40.4 us -> none  [per_device(): lax.psum_scatter(partial_value, 'tensor', scatter_dimension=1, tiled=True)]
    and x48 -> x0, other arithmetic: 9.73 us -> none  [block_mask(): (own_segment[:, None] == segment_block[None, :]) & (order_block[None, :]...]
  transfers between devices with their start and end apart: 5 -> 0, of which waited for: 4 -> 0; matrix products, arithmetic and copies ran while one was open for 10% -> 0% of each run, Pallas kernels for 0% -> 0%
where the time goes in v1:
time: 89 us; the launch traced here: 88.3 us
  Pallas kernels  78.8 us (89%)
  local copies, waits for them, and re-layouts  8.87 us (10%)
    pallas_call x1, Pallas kernels, per_device(): pl.pallas_call(functools.partial(kernel, nx, nz, ny, docs), out_shape=[ja...  78.8 us
    unnamed x18, local copies, waits for them, and re-layouts  8.87 us

profile of v1, /device:TPU:24, one launch (start us, length us, event | category | flops | bytes accessed | tf_op | source)
XLA Modules:
  0.0 88.3 jit_solution(1148718311308834892)
XLA Ops:
  0.6 0.0 copy-start
  0.6 1.6 %copy-done = bf16[256,4096]{1,0:T(8,128)(2,1)S(1)} copy-done((bf16[256,4096]{1,0:T(8,128)(2,1)S(1)}, bf16[256,4096]{1,0:T(8,128)(2,1)}, u32[]{:S(2)}) %copy-start) | copy-done | bytes 2097176
  2.2 0.0 copy-start.1
  2.2 0.9 %copy-done.1 = bf16[128,512]{1,0:T(8,128)(2,1)S(1)} copy-done((bf16[128,512]{1,0:T(8,128)(2,1)S(1)}, bf16[128,512]{1,0:T(8,128)(2,1)}, u32[]{:S(2)}) %copy-start.1) | copy-done | bytes 131096
  3.1 0.0 copy-start.2
  3.1 0.8 copy-done.2
  4.0 0.0 copy-start.3
  4.0 0.8 copy-done.3
  4.7 0.0 copy-start.4
  4.7 0.8 copy-done.4
  5.5 0.0 copy-start.5
  5.5 0.8 copy-done.5
  6.2 0.0 copy-start.6
  6.2 0.8 copy-done.6
  7.0 78.8 %shard_map.102 = (bf16[128,512]{1,0:T(8,128)(2,1)S(1)}, bf16[128,256]{1,0:T(8,128)(2,1)S(1)}, bf16[128,128]{1,0:T(8,128)(2,1)S(1)}, bf16[128,128]{1,0:T(8,128)(2,1)S(1)}) custom-call(bf16[128,256]{1,0:T(8,128)(2,1)S(1)} %copy-done.2, bf16[128,128]{1,0:T(8,128)(2,1)S(1)} %copy-done.3, bf16[128,128]{1,0:T(8,128)(2,1)S(1)} %copy-done.4, ...), custom_call_target="tpu_custom_call" | custom-call | flops 3758096384 | bytes 4194304 | tf_op jit(solution)/shard_map/pallas_call | solution.py:486
  85.8 0.7 copy.15
  86.5 0.6 copy.16
  87.1 0.6 copy.17
  87.7 0.6 copy.18
Async XLA Ops:
  0.6 1.6 %copy-start = (bf16[256,4096]{1,0:T(8,128)(2,1)S(1)}, bf16[256,4096]{1,0:T(8,128)(2,1)}, u32[]{:S(2)}) copy-start(bf16[256,4096]{1,0:T(8,128)(2,1)} %w_hbm.1) | copy-start | bytes 6291460
  2.2 0.9 %copy-start.1 = (bf16[128,512]{1,0:T(8,128)(2,1)S(1)}, bf16[128,512]{1,0:T(8,128)(2,1)}, u32[]{:S(2)}) copy-start(bf16[128,512]{1,0:T(8,128)(2,1)} %g_hbm.1) | copy-start | bytes 393220
  3.1 0.8 copy-start.2
  4.0 0.8 copy-start.3
  4.7 0.8 copy-start.4
  5.5 0.8 copy-start.5
  6.2 0.8 copy-start.6

commit v2 on v1

v2 whole, which is shorter than its diff:
```python
import functools
import math

import jax
import jax.numpy as jnp
from jax import lax
from jax.experimental import pallas as pl
from jax.experimental.pallas import tpu as pltpu
from jax.sharding import PartitionSpec as P

MESH = pl.DeviceIdType.MESH
NEG = -1e30
HD = 128
ROWS = 128
HEADS = 2
BF = jnp.bfloat16
F32 = jnp.float32
FACTORS = {64: (4, 16)}
PARENT = {3: 0, 1: 0, 6: 3, 2: 3, 4: 3, 5: 6, 7: 6, 8: 6}
LEAVES = (1, 2, 4, 5, 7, 8)
SIGNS = {(False, 0): (1, -1), (False, 1): (1, -1), (True, 0): (1,), (True, 1): (-1,)}

NN = (((1,), (0,)), ((), ()))
NT = (((1,), (1,)), ((), ()))
TN = (((0,), (0,)), ((), ()))


def mm(a, b, dims):
    return lax.dot_general(a, b, dims, preferred_element_type=F32)


def at128(index):
    return pl.ds(pl.multiple_of(index * 128, 128), 128)


def at256(index):
    return pl.ds(pl.multiple_of(index * 256, 256), 256)


def kernel(
    nx, nz, ny, docs,
    q_hbm, k_hbm, v_hbm, w_hbm, g_hbm, order_hbm, segment_hbm,
    out_hbm, dq_hbm, dk_hbm, dv_hbm,
    q_own, w, order, segment, kbuf, vbuf, q_t, do_t, g_all,
    pos_row, pos_key, scores, probs, dscores, top, total, o_t, dq_t,
    stats, inners, o_send, o_recv, factor, delta, fdo_t, fq_t,
    dk_part, dv_part, rs_send, rs_recv, dq_send, dq_recv,
    part_own, part_send, part_recv, y_send, y_recv,
    out_v, dq_v, dk_v, dv_v,
    in_sem, out_sem, kv_s, kv_r, q_s, q_r, do_s, do_r, st_s, st_r, in_s, in_r, o_s, o_r, dq_s, dq_r,
    gy_s, gy_r, gc_s, gc_r, pc_s, pc_r, py_s, py_r, rs_s, rs_r,
):
    context, tensor = lax.axis_index("context"), lax.axis_index("tensor")
    x, z = context // nz, lax.rem(context, nz)
    y, core = tensor // 2, lax.rem(tensor, 2)
    exponent = math.log2(math.e) / math.sqrt(HD)
    scale = 1.0 / math.sqrt(HD)
    slots = nx * HEADS
    width = slots * 128
    keys = nz * ROWS
    features = g_hbm.shape[1]
    x_at = [lax.rem(x + d, nx) for d in range(nx)]
    x_peer = [(x_at[d] * nz + z, tensor) for d in range(nx)]
    y_at = [lax.rem(y + d, ny) for d in range(ny)]
    y_peer = [(context, y_at[d] * 2 + core) for d in range(ny)]
    partner = (context, y * 2 + 1 - core)

    def z_at(offset):
        return lax.rem(z + offset + 2 * nz, nz)

    def z_peer(offset):
        return (x * nz + z_at(offset), tensor)

    def remote(src, dst, send, recv, device):
        return pltpu.make_async_remote_copy(
            src_ref=src, dst_ref=dst, send_sem=send, recv_sem=recv, device_id=device, device_id_type=MESH
        )

    load_q = pltpu.make_async_copy(q_hbm, q_own, in_sem.at[0])
    load_order = pltpu.make_async_copy(order_hbm, order, in_sem.at[1])
    load_segment = pltpu.make_async_copy(segment_hbm, segment, in_sem.at[2])
    load_k = pltpu.make_async_copy(k_hbm, kbuf.at[at128(z)], in_sem.at[3])
    load_v = pltpu.make_async_copy(v_hbm, vbuf.at[at128(z)], in_sem.at[4])
    load_g = pltpu.make_async_copy(g_hbm, g_all.at[tensor], in_sem.at[5])
    load_w = pltpu.make_async_copy(w_hbm, w, in_sem.at[6])

    barrier = pltpu.get_barrier_semaphore()
    peers = [z_peer(d) for d in (1, -1, 2, -2, 3, -3)] + x_peer[1:] + y_peer[1:] + [partner]
    for peer in peers:
        pl.semaphore_signal(barrier, inc=1, device_id=peer, device_id_type=MESH)
    for load in (load_q, load_order, load_segment, load_k, load_v, load_g, load_w):
        load.start()

    load_q.wait()
    for h in range(HEADS):
        q_t[:, at128(x * HEADS + h)] = q_own[:, h * HD : (h + 1) * HD].T

    pl.semaphore_wait(barrier, len(peers))

    def kv_copy(stream, sign, far):
        near = PARENT[far]
        src, buf = ((k_hbm, kbuf), (v_hbm, vbuf))[stream]
        slot = buf.at[at128(z_at(-sign * near))]
        at = sign * far + 8
        return remote(src if near == 0 else slot, slot, kv_s.at[stream, at], kv_r.at[stream, at], z_peer(sign * (far - near)))

    def kv_start(stream, *fars):
        for far in fars:
            for sign in SIGNS[far == 8, stream]:
                kv_copy(stream, sign, far).start()

    def kv_wait(stream, *fars):
        for far in fars:
            for sign in SIGNS[far == 8, stream]:
                kv_copy(stream, sign, far).wait_recv()

    def both(fn):
        @pl.loop(0, 2)
        def _(j):
            fn(1 - 2 * j)

    def q_copy(d):
        slot = q_t.at[:, at256(x)]
        return remote(slot, slot, q_s.at[d], q_r.at[d], x_peer[d])

    def do_copy(d):
        slot = do_t.at[:, at256(x)]
        return remote(slot, slot, do_s.at[d], do_r.at[d], x_peer[d])

    def gy_copy(d):
        return remote(g_hbm, g_all.at[tensor], gy_s.at[d], gy_r.at[d], y_peer[d])

    def gc_copy(d):
        at = y_at[d] * 2 + core
        return remote(g_hbm if d == 0 else g_all.at[at], g_all.at[at], gc_s.at[d], gc_r.at[d], partner)

    kv_start(0, 3, 1)
    for d in range(1, nx):
        q_copy(d).start()
    for d in range(1, ny):
        gy_copy(d).start()
    gc_copy(0).start()
    kv_start(1, 3, 1)

    load_order.wait()
    load_segment.wait()
    starts = [
        jnp.sum(jnp.where(segment[...] < d, 1, 0), axis=(0, 1), keepdims=True) for d in range(1, docs)
    ]
    for xp in range(nx):
        own = order[pl.ds(xp * nz + z, 1), :]
        first = jnp.zeros_like(own)
        for start in starts:
            first = jnp.maximum(first, jnp.where(start <= own, start, 0))
        pos_row[xp : xp + 1, :] = own
        pos_row[nx + xp : nx + xp + 1, :] = first

    @pl.loop(0, nz)
    def _(b):
        row = order[pl.ds(x * nz + b, 1), :]
        pos_key[at128(b), :] = jnp.broadcast_to(row, (ROWS, 128)).T

    top[...] = jnp.full_like(top, NEG)

    def score_block(b):
        raw = mm(kbuf[at128(b), :], q_t[...], NN)
        key = pos_key[at128(b), :]
        for xp in range(nx):
            mask = (key >= pos_row[nx + xp : nx + xp + 1, :]) & (key <= pos_row[xp : xp + 1, :])
            for h in range(HEADS):
                lanes = slice((xp * HEADS + h) * 128, (xp * HEADS + h + 1) * 128)
                part = jnp.where(mask, raw[:, lanes], NEG)
                scores[at128(b), lanes] = part
                top[:, lanes] = jnp.maximum(top[:, lanes], jnp.max(part.reshape(ROWS // 8, 8, 128), axis=0))

    def score_far(*fars, wait=True):
        def one(sign):
            for far in fars:
                if wait:
                    kv_copy(0, sign, far).wait_recv()
                score_block(z_at(-sign * far))

        both(one)

    def cotangent_relay():
        for d in range(1, ny):
            gy_copy(d).wait_recv()
        for d in range(1, ny):
            gc_copy(d).start()

    def cotangent():
        load_w.wait()
        load_g.wait()
        for d in range(ny):
            gc_copy(d).wait_recv()
        acc = jnp.zeros((HEADS * HD, ROWS), F32)
        for t in range(2 * ny):
            acc = acc + mm(w[:, t * features : (t + 1) * features], g_all[t], NT)
        for h in range(HEADS):
            do_t[:, at128(x * HEADS + h)] = acc[h * HD : (h + 1) * HD, :].astype(BF)
        for d in range(1, nx):
            do_copy(d).start()

    kv_wait(0, 3)
    kv_start(0, 6, 2, 4)
    load_k.wait()
    for d in range(1, nx):
        q_copy(d).wait_recv()
    score_block(z)
    score_far(3, wait=False)
    kv_wait(1, 3)
    kv_start(1, 6, 2, 4)
    score_far(1)
    kv_wait(0, 6)
    kv_start(0, 5, 7, 8)
    cotangent_relay()
    score_far(6, wait=False)
    score_far(2, 4)
    kv_wait(1, 6)
    kv_start(1, 5, 7, 8)
    cotangent()
    score_far(5, 7)
    kv_wait(0, 8)
    score_block(z_at(-8))

    peak = jnp.max(top[...], axis=0, keepdims=True)
    total[...] = jnp.zeros_like(total)

    @pl.loop(0, nz)
    def _(i):
        p = jnp.exp2((scores[at128(i), :] - peak) * exponent)
        probs[at128(i), :] = p.astype(BF)
        total[...] += jnp.sum(p.reshape(16, 8, width), axis=0)

    sums = jnp.sum(total[...], axis=0, keepdims=True)
    for s in range(slots):
        lanes = slice(s * 128, (s + 1) * 128)
        stats[x, 0, s : s + 1, :] = peak[:, lanes]
        stats[x, 1, s : s + 1, :] = sums[:, lanes]

    def st_copy(d):
        return remote(stats.at[x], stats.at[x], st_s.at[d], st_r.at[d], x_peer[d])

    def in_copy(d):
        return remote(inners.at[x], inners.at[x], in_s.at[d], in_r.at[d], x_peer[d])

    def o_copy(d):
        return remote(o_send.at[:, at256(x_at[d])], o_recv.at[d], o_s.at[d], o_r.at[d], x_peer[d])

    for d in range(1, nx):
        st_copy(d).start()
    for d in range(1, nx):
        do_copy(d).wait_recv()
    for d in range(1, nx):
        st_copy(d).wait_recv()

    peak_all = functools.reduce(jnp.maximum, [stats[i, 0] for i in range(nx)])
    weight = [jnp.exp2((stats[i, 0] - peak_all) * exponent) for i in range(nx)]
    inverse = 1.0 / functools.reduce(jnp.add, [weight[i] * stats[i, 1] for i in range(nx)])
    for i in range(nx):
        factor[i] = weight[i] * inverse
    mine = factor[x]
    for s in range(slots):
        lanes = slice(s * 128, (s + 1) * 128)
        f = mine[s : s + 1, :]
        fdo_t[:, lanes] = (do_t[:, lanes].astype(F32) * f).astype(BF)
        fq_t[:, lanes] = (q_t[:, lanes].astype(F32) * (f * scale)).astype(BF)

    def rs_copy(stream, sign, far):
        at = sign * far + 8
        return remote(
            rs_send.at[stream, at], rs_recv.at[stream, at], rs_s.at[stream, at], rs_r.at[stream, at],
            z_peer(sign * (PARENT[far] - far)),
        )

    def rs_out(stream, sign, far, *kids):
        acc = (dk_part, dv_part)[stream][z_at(-sign * far)]
        for kid in kids:
            rs_copy(stream, sign, kid).wait_recv()
            acc = acc + rs_recv[stream, sign * kid + 8].astype(F32)
        rs_send[stream, sign * far + 8] = acc.astype(BF)
        rs_copy(stream, sign, far).start()

    def rs_hubs(stream, far):
        for sign in (1, -1):
            kids = (2, 4, 6) if far == 3 else (5, 7, 8) if sign in SIGNS[True, stream] else (5, 7)
            rs_out(stream, sign, far, *kids)

    def dv_block(b):
        dv_part[b] = mm(probs[at128(b), :], fdo_t[...], NT)

    def ds_block(b):
        dp = mm(vbuf[at128(b), :], do_t[...], NN)
        for s in range(slots):
            lanes = slice(s * 128, (s + 1) * 128)
            p = probs[at128(b), lanes].astype(F32)
            dscores[at128(b), lanes] = (p * (dp[:, lanes] - delta[s : s + 1, :])).astype(BF)
        ds = dscores[at128(b), :]
        dk_part[b] = mm(ds, fq_t[...], NT)
        dq_t[...] += mm(kbuf[at128(b), :], ds, TN)

    def grad_far(stream, *fars):
        block = (ds_block, dv_block)[stream]

        def one(sign):
            for far in fars:
                block(z_at(-sign * far))
                if far in LEAVES:
                    rs_out(stream, sign, far)

        both(one)

    def grad_antipode(stream):
        (ds_block, dv_block)[stream](z_at(-8))
        rs_out(stream, SIGNS[True, stream][0], 8)

    grad_far(1, 5, 7)
    grad_antipode(1)
    grad_far(1, 2, 4)
    grad_far(1, 1, 6, 3)
    dv_block(z)

    load_v.wait()
    kv_wait(1, 1, 2, 4, 5, 7, 8)
    o_t[...] = jnp.zeros_like(o_t)
    chunk = min(512, keys)

    @pl.loop(0, keys // chunk)
    def _(i):
        at = pl.ds(pl.multiple_of(i * chunk, chunk), chunk)
        o_t[...] += mm(vbuf[at, :], probs[at, :], TN)

    inner = jnp.sum(o_t[...] * do_t[...].astype(F32), axis=0, keepdims=True)
    for s in range(slots):
        inners[x, s : s + 1, :] = inner[:, s * 128 : (s + 1) * 128]
    for d in range(1, nx):
        in_copy(d).start()
    o_send[...] = o_t[...].astype(BF)
    for d in range(1, nx):
        o_copy(d).start()
    rs_hubs(1, 6)
    dq_t[...] = jnp.zeros_like(dq_t)
    for d in range(1, nx):
        in_copy(d).wait_recv()
    delta[...] = functools.reduce(jnp.add, [factor[i] * inners[i] for i in range(nx)])

    def dq_copy(d):
        return remote(dq_send.at[:, at256(x_at[d])], dq_recv.at[d], dq_s.at[d], dq_r.at[d], x_peer[d])

    def pc_copy():
        return remote(part_send, part_recv, pc_s.at[0], pc_r.at[0], partner)

    def py_copy(d):
        return remote(y_send.at[y_at[d]], y_recv.at[d], py_s.at[d], py_r.at[d], y_peer[d])

    def project():
        for d in range(1, nx):
            o_copy(d).wait_recv()
        attended = []
        for h in range(HEADS):
            acc = o_send[:, at128(x * HEADS + h)].astype(F32) * factor[x, pl.ds(x * HEADS + h, 1), :]
            for d in range(1, nx):
                source = lax.rem(x - d + nx, nx)
                acc = acc + (
                    o_recv[d, :, h * 128 : (h + 1) * 128].astype(F32) * factor[source, pl.ds(x * HEADS + h, 1), :]
                )
            attended.append(acc.astype(BF))
        attended = jnp.concatenate(attended, axis=0)

        @pl.loop(0, ny)
        def _(yp):
            for c in range(2):
                at = pl.ds(pl.multiple_of((yp * 2 + c) * features, features), features)
                part = mm(attended, w[:, at], TN)

                @pl.when(core == c)
                def _():
                    part_own[yp] = part

                @pl.when(core != c)
                def _():
                    part_send[yp] = part.astype(BF)

        pc_copy().start()

    def spread():
        pc_copy().wait_recv()

        @pl.loop(0, ny)
        def _(yp):
            part = part_own[yp] + part_recv[yp].astype(F32)
            part_own[yp] = part
            y_send[yp] = part.astype(BF)

        for d in range(1, ny):
            py_copy(d).start()

    def send_dq():
        for s in range(slots):
            lanes = slice(s * 128, (s + 1) * 128)
            dq_t[:, lanes] = dq_t[:, lanes] * (factor[x, s : s + 1, :] * scale)
        dq_send[...] = dq_t[...].astype(BF)
        for d in range(1, nx):
            dq_copy(d).start()

    grad_far(0, 5, 7)
    grad_antipode(0)
    grad_far(0, 2, 4)
    rs_hubs(1, 3)
    project()
    grad_far(0, 1, 6, 3)
    ds_block(z)
    rs_hubs(0, 6)
    spread()
    send_dq()
    rs_hubs(0, 3)

    def owned(part, stream):
        acc = part[z]
        for far in (1, 3):
            for sign in (1, -1):
                rs_copy(stream, sign, far).wait_recv()
                acc = acc + rs_recv[stream, sign * far + 8].astype(F32)
        return acc.astype(BF)

    dv_v[...] = owned(dv_part, 1)
    store_dv = pltpu.make_async_copy(dv_v, dv_hbm, out_sem.at[2])
    store_dv.start()
    for d in range(1, nx):
        dq_copy(d).wait_recv()
    for h in range(HEADS):
        acc = dq_t[:, at128(x * HEADS + h)]
        for d in range(1, nx):
            acc = acc + dq_recv[d, :, h * 128 : (h + 1) * 128].astype(F32)
        dq_v[:, h * 128 : (h + 1) * 128] = acc.T.astype(BF)
    store_dq = pltpu.make_async_copy(dq_v, dq_hbm, out_sem.at[1])
    store_dq.start()
    for d in range(1, ny):
        py_copy(d).wait_recv()
    out = part_own[y]
    for d in range(1, ny):
        out = out + y_recv[d].astype(F32)
    out_v[...] = out.astype(BF)
    store_out = pltpu.make_async_copy(out_v, out_hbm, out_sem.at[0])
    store_out.start()
    dk_v[...] = owned(dk_part, 0)
    store_dk = pltpu.make_async_copy(dk_v, dk_hbm, out_sem.at[3])
    store_dk.start()

    for stream in range(2):
        for far in PARENT:
            for sign in SIGNS[far == 8, stream]:
                kv_copy(stream, sign, far).wait_send()
                rs_copy(stream, sign, far).wait_send()
    for d in range(1, nx):
        for copy in (q_copy, do_copy, st_copy, in_copy, o_copy, dq_copy):
            copy(d).wait_send()
    for d in range(1, ny):
        gy_copy(d).wait_send()
        py_copy(d).wait_send()
    for d in range(ny):
        gc_copy(d).wait_send()
    pc_copy().wait_send()
    for store in (store_out, store_dq, store_dv, store_dk):
        store.wait()


def per_device(nx, nz, ny, docs, query, key_proj, value, out_weight, grad_out, order, segment):
    features = grad_out.shape[1]
    keys, width, slots = nz * ROWS, nx * HEADS * 128, nx * HEADS
    tokens = order.shape[0]
    order = order.reshape(tokens // 128, 128)
    segment = segment.reshape(tokens // 128, 128)

    def vm(*shape, dtype=BF):
        return pltpu.VMEM(shape, dtype)

    def sem(*shape):
        return pltpu.SemaphoreType.DMA(shape)

    scratch = [
        vm(ROWS, HEADS * HD), vm(HEADS * HD, out_weight.shape[1]),
        vm(tokens // 128, 128, dtype=jnp.int32), vm(tokens // 128, 128, dtype=jnp.int32),
        vm(keys, HD), vm(keys, HD), vm(HD, width), vm(HD, width), vm(2 * ny, ROWS, features),
        vm(2 * nx, 128, dtype=jnp.int32), vm(keys, 128, dtype=jnp.int32),
        vm(keys, width, dtype=F32), vm(keys, width), vm(keys, width),
        vm(8, width, dtype=F32), vm(8, width, dtype=F32), vm(HD, width, dtype=F32), vm(HD, width, dtype=F32),
        vm(nx, 2, slots, 128, dtype=F32), vm(nx, slots, 128, dtype=F32), vm(HD, width), vm(nx, HD, 256),
        vm(nx, slots, 128, dtype=F32), vm(slots, 128, dtype=F32), vm(HD, width), vm(HD, width),
        vm(nz, ROWS, HD, dtype=F32), vm(nz, ROWS, HD, dtype=F32),
        vm(2, 17, ROWS, HD), vm(2, 17, ROWS, HD), vm(HD, width), vm(nx, HD, 256),
        vm(ny, ROWS, features, dtype=F32), vm(ny, ROWS, features), vm(ny, ROWS, features),
        vm(ny, ROWS, features), vm(ny, ROWS, features),
        vm(ROWS, features), vm(ROWS, HEADS * HD), vm(ROWS, HD), vm(ROWS, HD),
        sem(7), sem(4), sem(2, 17), sem(2, 17),
    ] + [sem(nx)] * 12 + [sem(ny)] * 4 + [sem(1)] * 2 + [sem(ny)] * 2 + [sem(2, 17)] * 2
    flops = 2 * width * keys * HD * 6 + 4 * ROWS * HEADS * HD * out_weight.shape[1]
    return pl.pallas_call(
        functools.partial(kernel, nx, nz, ny, docs),
        out_shape=[
            jax.ShapeDtypeStruct((ROWS, features), BF),
            jax.ShapeDtypeStruct((ROWS, HEADS * HD), BF),
            jax.ShapeDtypeStruct((ROWS, HD), BF),
            jax.ShapeDtypeStruct((ROWS, HD), BF),
        ],
        in_specs=[pl.BlockSpec(memory_space=pl.ANY)] * 7,
        out_specs=[pl.BlockSpec(memory_space=pl.ANY)] * 4,
        scratch_shapes=scratch,
        compiler_params=pltpu.CompilerParams(
            collective_id=0, has_side_effects=True, vmem_limit_bytes=60 * 1024 * 1024
        ),
        cost_estimate=pl.CostEstimate(flops=flops, bytes_accessed=4 << 20, transcendentals=keys * width),
    )(query, key_proj, value, out_weight, grad_out, order, segment)


def solution(mesh):
    nx, nz = FACTORS[mesh.shape["context"]]
    ny = mesh.shape["tensor"] // 2
    return jax.shard_map(
        functools.partial(per_device, nx, nz, ny, 8),
        mesh=mesh,
        in_specs=(
            P("context", "tensor"),
            P("context", "tensor"),
            P("context", "tensor"),
            P("tensor", None),
            P("context", "tensor"),
            P(),
            P(),
        ),
        out_specs=(P("context", "tensor"),) * 4,
        check_vma=False,
    )
```

time: 89 us -> 73 us (0.82)
  Pallas kernels: 78.8 us -> 65.9 us
  local copies, waits for them, and re-layouts: 8.87 us -> 5.79 us
    pallas_call x1, Pallas kernels: 78.8 us -> 65.9 us  [per_device(): pl.pallas_call(functools.partial(kernel, nx, nz, ny, docs), out_shape=[ja...]
    unnamed x18 -> x4, local copies, waits for them, and re-layouts: 8.87 us -> 5.79 us
where the time goes in v2:
time: 73 us; the launch traced here: 72.3 us
  Pallas kernels  65.9 us (90%)
  local copies, waits for them, and re-layouts  5.79 us (8%)
    pallas_call x1, Pallas kernels, per_device(): pl.pallas_call(functools.partial(kernel, nx, nz, ny, docs), out_shape=[ja...  65.9 us
    unnamed x4, local copies, waits for them, and re-layouts  5.79 us

profile of v2, /device:TPU:24, one launch (start us, length us, event | category | flops | bytes accessed | tf_op | source)
XLA Modules:
  0.0 72.3 jit_solution(11799184013935613584)
XLA Ops:
  0.6 65.9 %shard_map.102 = (bf16[128,512]{1,0:T(8,128)(2,1)}, bf16[128,256]{1,0:T(8,128)(2,1)}, bf16[128,128]{1,0:T(8,128)(2,1)}, bf16[128,128]{1,0:T(8,128)(2,1)}) custom-call(bf16[128,256]{1,0:T(8,128)(2,1)} %q_hbm.1, bf16[128,128]{1,0:T(8,128)(2,1)} %k_hbm.1, bf16[128,128]{1,0:T(8,128)(2,1)} %v_hbm.1, bf16[256,4096]{1,0:T(8,128)(2,1)} %w_hbm.1, ...), custom_call_target="tpu_custom_call" | custom-call | flops 3758096384 | bytes 4194304 | tf_op jit(solution)/shard_map/pallas_call | solution.py:498
  66.6 1.6 %copy.15 = bf16[128,512]{1,0:T(8,128)(2,1)} copy(bf16[128,512]{1,0:T(8,128)(2,1)} %get-tuple-element.8) | data formatting | bytes 262144
  68.1 1.5 %copy.16 = bf16[128,256]{1,0:T(8,128)(2,1)} copy(bf16[128,256]{1,0:T(8,128)(2,1)} %get-tuple-element.9) | data formatting | bytes 131072
  69.6 1.4 %copy.17 = bf16[128,128]{1,0:T(8,128)(2,1)} copy(bf16[128,128]{1,0:T(8,128)(2,1)} %get-tuple-element.10) | data formatting | bytes 65536
  71.0 1.4 %copy.18 = bf16[128,128]{1,0:T(8,128)(2,1)} copy(bf16[128,128]{1,0:T(8,128)(2,1)} %get-tuple-element.11) | data formatting | bytes 65536

commit v3 on v2

--- a/solution.py
+++ b/solution.py
@@ -17,6 +17,7 @@
 F32 = jnp.float32
 FACTORS = {64: (4, 16)}
 PARENT = {3: 0, 1: 0, 6: 3, 2: 3, 4: 3, 5: 6, 7: 6, 8: 6}
+UP = (PARENT, PARENT)
 LEAVES = (1, 2, 4, 5, 7, 8)
 SIGNS = {(False, 0): (1, -1), (False, 1): (1, -1), (True, 0): (1,), (True, 1): (-1,)}
 
@@ -40,14 +41,13 @@
 def kernel(
     nx, nz, ny, docs,
     q_hbm, k_hbm, v_hbm, w_hbm, g_hbm, order_hbm, segment_hbm,
-    out_hbm, dq_hbm, dk_hbm, dv_hbm,
+    out_v, dq_v, dk_v, dv_v,
     q_own, w, order, segment, kbuf, vbuf, q_t, do_t, g_all,
     pos_row, pos_key, scores, probs, dscores, top, total, o_t, dq_t,
     stats, inners, o_send, o_recv, factor, delta, fdo_t, fq_t,
     dk_part, dv_part, rs_send, rs_recv, dq_send, dq_recv,
     part_own, part_send, part_recv, y_send, y_recv,
-    out_v, dq_v, dk_v, dv_v,
-    in_sem, out_sem, kv_s, kv_r, q_s, q_r, do_s, do_r, st_s, st_r, in_s, in_r, o_s, o_r, dq_s, dq_r,
+    in_sem, kv_s, kv_r, q_s, q_r, do_s, do_r, st_s, st_r, in_s, in_r, o_s, o_r, dq_s, dq_r,
     gy_s, gy_r, gc_s, gc_r, pc_s, pc_r, py_s, py_r, rs_s, rs_r,
 ):
     context, tensor = lax.axis_index("context"), lax.axis_index("tensor")
@@ -91,10 +91,6 @@
     for load in (load_q, load_order, load_segment, load_k, load_v, load_g, load_w):
         load.start()
 
-    load_q.wait()
-    for h in range(HEADS):
-        q_t[:, at128(x * HEADS + h)] = q_own[:, h * HD : (h + 1) * HD].T
-
     pl.semaphore_wait(barrier, len(peers))
 
     def kv_copy(stream, sign, far):
@@ -114,10 +110,12 @@
             for sign in SIGNS[far == 8, stream]:
                 kv_copy(stream, sign, far).wait_recv()
 
-    def both(fn):
-        @pl.loop(0, 2)
-        def _(j):
-            fn(1 - 2 * j)
+    def kv_relay(stream, far, *kids):
+        for sign in (1, -1):
+            kv_copy(stream, sign, far).wait_recv()
+            for kid in kids:
+                if sign in SIGNS[kid == 8, stream]:
+                    kv_copy(stream, sign, kid).start()
 
     def q_copy(d):
         slot = q_t.at[:, at256(x)]
@@ -134,12 +132,16 @@
         at = y_at[d] * 2 + core
         return remote(g_hbm if d == 0 else g_all.at[at], g_all.at[at], gc_s.at[d], gc_r.at[d], partner)
 
-    kv_start(0, 3, 1)
-    for d in range(1, nx):
-        q_copy(d).start()
+    kv_start(0, 3)
     for d in range(1, ny):
         gy_copy(d).start()
     gc_copy(0).start()
+    load_q.wait()
+    for h in range(HEADS):
+        q_t[:, at128(x * HEADS + h)] = q_own[:, h * HD : (h + 1) * HD].T
+    for d in range(1, nx):
+        q_copy(d).start()
+    kv_start(0, 1)
     kv_start(1, 3, 1)
 
     load_order.wait()
@@ -162,25 +164,29 @@
 
     top[...] = jnp.full_like(top, NEG)
 
-    def score_block(b):
-        raw = mm(kbuf[at128(b), :], q_t[...], NN)
-        key = pos_key[at128(b), :]
-        for xp in range(nx):
-            mask = (key >= pos_row[nx + xp : nx + xp + 1, :]) & (key <= pos_row[xp : xp + 1, :])
-            for h in range(HEADS):
-                lanes = slice((xp * HEADS + h) * 128, (xp * HEADS + h + 1) * 128)
-                part = jnp.where(mask, raw[:, lanes], NEG)
-                scores[at128(b), lanes] = part
-                top[:, lanes] = jnp.maximum(top[:, lanes], jnp.max(part.reshape(ROWS // 8, 8, 128), axis=0))
+    def stacked(ref, blocks):
+        return jnp.concatenate([ref[at128(b), :] for b in blocks], axis=0)
+
+    def score_blocks(*blocks):
+        raw = mm(stacked(kbuf, blocks), q_t[...], NN)
+        for i, b in enumerate(blocks):
+            key = pos_key[at128(b), :]
+            for xp in range(nx):
+                mask = (key >= pos_row[nx + xp : nx + xp + 1, :]) & (key <= pos_row[xp : xp + 1, :])
+                for h in range(HEADS):
+                    lanes = slice((xp * HEADS + h) * 128, (xp * HEADS + h + 1) * 128)
+                    part = jnp.where(mask, raw[i * ROWS : (i + 1) * ROWS, lanes], NEG)
+                    scores[at128(b), lanes] = part
+                    top[:, lanes] = jnp.maximum(top[:, lanes], jnp.max(part.reshape(ROWS // 8, 8, 128), axis=0))
+
+    def sides(far):
+        return z_at(-far), z_at(far)
 
     def score_far(*fars, wait=True):
-        def one(sign):
-            for far in fars:
-                if wait:
-                    kv_copy(0, sign, far).wait_recv()
-                score_block(z_at(-sign * far))
-
-        both(one)
+        for far in fars:
+            if wait:
+                kv_wait(0, far)
+            score_blocks(*sides(far))
 
     def cotangent_relay():
         for d in range(1, ny):
@@ -201,27 +207,23 @@
         for d in range(1, nx):
             do_copy(d).start()
 
-    kv_wait(0, 3)
-    kv_start(0, 6, 2, 4)
+    kv_relay(0, 3, 6, 2, 4)
     load_k.wait()
     for d in range(1, nx):
         q_copy(d).wait_recv()
-    score_block(z)
+    kv_relay(1, 3, 6, 2, 4)
+    score_blocks(z)
     score_far(3, wait=False)
-    kv_wait(1, 3)
-    kv_start(1, 6, 2, 4)
     score_far(1)
-    kv_wait(0, 6)
-    kv_start(0, 5, 7, 8)
     cotangent_relay()
+    kv_relay(0, 6, 5, 7, 8)
     score_far(6, wait=False)
-    score_far(2, 4)
-    kv_wait(1, 6)
-    kv_start(1, 5, 7, 8)
+    score_far(2)
+    kv_relay(1, 6, 5, 7, 8)
     cotangent()
-    score_far(5, 7)
+    score_far(4, 5, 7)
     kv_wait(0, 8)
-    score_block(z_at(-8))
+    score_blocks(z_at(-8))
 
     peak = jnp.max(top[...], axis=0, keepdims=True)
     total[...] = jnp.zeros_like(total)
@@ -249,8 +251,26 @@
 
     for d in range(1, nx):
         st_copy(d).start()
+    load_v.wait()
+    kv_wait(1, 1, 2, 4, 5, 7, 8)
+    o_t[...] = jnp.zeros_like(o_t)
+    chunk = min(512, keys)
+
+    @pl.loop(0, keys // chunk)
+    def _(i):
+        at = pl.ds(pl.multiple_of(i * chunk, chunk), chunk)
+        o_t[...] += mm(vbuf[at, :], probs[at, :], TN)
+
     for d in range(1, nx):
         do_copy(d).wait_recv()
+    inner = jnp.sum(o_t[...] * do_t[...].astype(F32), axis=0, keepdims=True)
+    for s in range(slots):
+        inners[x, s : s + 1, :] = inner[:, s * 128 : (s + 1) * 128]
+    for d in range(1, nx):
+        in_copy(d).start()
+    o_send[...] = o_t[...].astype(BF)
+    for d in range(1, nx):
+        o_copy(d).start()
     for d in range(1, nx):
         st_copy(d).wait_recv()
 
@@ -270,7 +290,7 @@
         at = sign * far + 8
         return remote(
             rs_send.at[stream, at], rs_recv.at[stream, at], rs_s.at[stream, at], rs_r.at[stream, at],
-            z_peer(sign * (PARENT[far] - far)),
+            z_peer(sign * (UP[stream][far] - far)),
         )
 
     def rs_out(stream, sign, far, *kids):
@@ -283,62 +303,43 @@
 
     def rs_hubs(stream, far):
         for sign in (1, -1):
-            kids = (2, 4, 6) if far == 3 else (5, 7, 8) if sign in SIGNS[True, stream] else (5, 7)
-            rs_out(stream, sign, far, *kids)
-
-    def dv_block(b):
-        dv_part[b] = mm(probs[at128(b), :], fdo_t[...], NT)
-
-    def ds_block(b):
-        dp = mm(vbuf[at128(b), :], do_t[...], NN)
-        for s in range(slots):
-            lanes = slice(s * 128, (s + 1) * 128)
-            p = probs[at128(b), lanes].astype(F32)
-            dscores[at128(b), lanes] = (p * (dp[:, lanes] - delta[s : s + 1, :])).astype(BF)
-        ds = dscores[at128(b), :]
-        dk_part[b] = mm(ds, fq_t[...], NT)
-        dq_t[...] += mm(kbuf[at128(b), :], ds, TN)
+            kids = [kid for kid in UP[stream] if UP[stream][kid] == far]
+            rs_out(stream, sign, far, *[kid for kid in kids if sign in SIGNS[kid == 8, stream]])
+
+    def dv_blocks(*blocks):
+        part = mm(stacked(probs, blocks), fdo_t[...], NT)
+        for i, b in enumerate(blocks):
+            dv_part[b] = part[i * ROWS : (i + 1) * ROWS, :]
+
+    def ds_blocks(*blocks):
+        dp = mm(stacked(vbuf, blocks), do_t[...], NN)
+        for i, b in enumerate(blocks):
+            for s in range(slots):
+                lanes = slice(s * 128, (s + 1) * 128)
+                p = probs[at128(b), lanes].astype(F32)
+                diff = dp[i * ROWS : (i + 1) * ROWS, lanes] - delta[s : s + 1, :]
+                dscores[at128(b), lanes] = (p * diff).astype(BF)
+        ds = stacked(dscores, blocks)
+        part = mm(ds, fq_t[...], NT)
+        for i, b in enumerate(blocks):
+            dk_part[b] = part[i * ROWS : (i + 1) * ROWS, :]
+        dq_t[...] += mm(stacked(kbuf, blocks), ds, TN)
 
     def grad_far(stream, *fars):
-        block = (ds_block, dv_block)[stream]
-
-        def one(sign):
-            for far in fars:
-                block(z_at(-sign * far))
-                if far in LEAVES:
+        for far in fars:
+            (ds_blocks, dv_blocks)[stream](*sides(far))
+            if far in LEAVES:
+                for sign in (1, -1):
                     rs_out(stream, sign, far)
 
-        both(one)
-
     def grad_antipode(stream):
-        (ds_block, dv_block)[stream](z_at(-8))
+        (ds_blocks, dv_blocks)[stream](z_at(-8))
         rs_out(stream, SIGNS[True, stream][0], 8)
 
     grad_far(1, 5, 7)
     grad_antipode(1)
-    grad_far(1, 2, 4)
-    grad_far(1, 1, 6, 3)
-    dv_block(z)
-
-    load_v.wait()
-    kv_wait(1, 1, 2, 4, 5, 7, 8)
-    o_t[...] = jnp.zeros_like(o_t)
-    chunk = min(512, keys)
-
-    @pl.loop(0, keys // chunk)
-    def _(i):
-        at = pl.ds(pl.multiple_of(i * chunk, chunk), chunk)
-        o_t[...] += mm(vbuf[at, :], probs[at, :], TN)
-
-    inner = jnp.sum(o_t[...] * do_t[...].astype(F32), axis=0, keepdims=True)
-    for s in range(slots):
-        inners[x, s : s + 1, :] = inner[:, s * 128 : (s + 1) * 128]
-    for d in range(1, nx):
-        in_copy(d).start()
-    o_send[...] = o_t[...].astype(BF)
-    for d in range(1, nx):
-        o_copy(d).start()
-    rs_hubs(1, 6)
+    grad_far(1, 2, 4, 1, 6, 3)
+    dv_blocks(z)
     dq_t[...] = jnp.zeros_like(dq_t)
     for d in range(1, nx):
         in_copy(d).wait_recv()
@@ -405,27 +406,27 @@
 
     grad_far(0, 5, 7)
     grad_antipode(0)
+    rs_hubs(1, 6)
     grad_far(0, 2, 4)
+    project()
+    grad_far(0, 6)
+    rs_hubs(0, 6)
+    grad_far(0, 3, 1)
+    ds_blocks(z)
+    send_dq()
+    spread()
     rs_hubs(1, 3)
-    project()
-    grad_far(0, 1, 6, 3)
-    ds_block(z)
-    rs_hubs(0, 6)
-    spread()
-    send_dq()
     rs_hubs(0, 3)
 
     def owned(part, stream):
         acc = part[z]
-        for far in (1, 3):
+        for far in [far for far in UP[stream] if UP[stream][far] == 0]:
             for sign in (1, -1):
                 rs_copy(stream, sign, far).wait_recv()
                 acc = acc + rs_recv[stream, sign * far + 8].astype(F32)
         return acc.astype(BF)
 
     dv_v[...] = owned(dv_part, 1)
-    store_dv = pltpu.make_async_copy(dv_v, dv_hbm, out_sem.at[2])
-    store_dv.start()
     for d in range(1, nx):
         dq_copy(d).wait_recv()
     for h in range(HEADS):
@@ -433,19 +434,13 @@
         for d in range(1, nx):
             acc = acc + dq_recv[d, :, h * 128 : (h + 1) * 128].astype(F32)
         dq_v[:, h * 128 : (h + 1) * 128] = acc.T.astype(BF)
-    store_dq = pltpu.make_async_copy(dq_v, dq_hbm, out_sem.at[1])
-    store_dq.start()
     for d in range(1, ny):
         py_copy(d).wait_recv()
     out = part_own[y]
     for d in range(1, ny):
         out = out + y_recv[d].astype(F32)
     out_v[...] = out.astype(BF)
-    store_out = pltpu.make_async_copy(out_v, out_hbm, out_sem.at[0])
-    store_out.start()
     dk_v[...] = owned(dk_part, 0)
-    store_dk = pltpu.make_async_copy(dk_v, dk_hbm, out_sem.at[3])
-    store_dk.start()
 
     for stream in range(2):
         for far in PARENT:
@@ -461,8 +456,6 @@
     for d in range(ny):
         gc_copy(d).wait_send()
     pc_copy().wait_send()
-    for store in (store_out, store_dq, store_dv, store_dk):
-        store.wait()
 
 
 def per_device(nx, nz, ny, docs, query, key_proj, value, out_weight, grad_out, order, segment):
@@ -491,26 +484,26 @@
         vm(2, 17, ROWS, HD), vm(2, 17, ROWS, HD), vm(HD, width), vm(nx, HD, 256),
         vm(ny, ROWS, features, dtype=F32), vm(ny, ROWS, features), vm(ny, ROWS, features),
         vm(ny, ROWS, features), vm(ny, ROWS, features),
-        vm(ROWS, features), vm(ROWS, HEADS * HD), vm(ROWS, HD), vm(ROWS, HD),
-        sem(7), sem(4), sem(2, 17), sem(2, 17),
+        sem(7), sem(2, 17), sem(2, 17),
     ] + [sem(nx)] * 12 + [sem(ny)] * 4 + [sem(1)] * 2 + [sem(ny)] * 2 + [sem(2, 17)] * 2
+    args = (query, key_proj, value, out_weight, grad_out, order, segment)
     flops = 2 * width * keys * HD * 6 + 4 * ROWS * HEADS * HD * out_weight.shape[1]
     return pl.pallas_call(
         functools.partial(kernel, nx, nz, ny, docs),
         out_shape=[
-            jax.ShapeDtypeStruct((ROWS, features), BF),
-            jax.ShapeDtypeStruct((ROWS, HEADS * HD), BF),
-            jax.ShapeDtypeStruct((ROWS, HD), BF),
-            jax.ShapeDtypeStruct((ROWS, HD), BF),
+            pltpu.VMEM((ROWS, features), BF),
+            pltpu.VMEM((ROWS, HEADS * HD), BF),
+            pltpu.VMEM((ROWS, HD), BF),
+            pltpu.VMEM((ROWS, HD), BF),
         ],
-        in_specs=[pl.BlockSpec(memory_space=pl.ANY)] * 7,
-        out_specs=[pl.BlockSpec(memory_space=pl.ANY)] * 4,
+        in_specs=[pl.BlockSpec(memory_space=pltpu.HBM)] * 7,
+        out_specs=[pl.BlockSpec(memory_space=pltpu.VMEM)] * 4,
         scratch_shapes=scratch,
         compiler_params=pltpu.CompilerParams(
-            collective_id=0, has_side_effects=True, vmem_limit_bytes=60 * 1024 * 1024
+            collective_id=0, has_side_effects=True, vmem_limit_bytes=56 * 1024 * 1024
         ),
         cost_estimate=pl.CostEstimate(flops=flops, bytes_accessed=4 << 20, transcendentals=keys * width),
-    )(query, key_proj, value, out_weight, grad_out, order, segment)
+    )(*[pltpu.with_memory_space_constraint(a, pltpu.HBM) for a in args])
 
 
 def solution(mesh):

time: 73 us -> 65 us (0.89)
  Pallas kernels: 65.9 us -> 61.2 us
  local copies, waits for them, and re-layouts: 5.79 us -> 2.52 us
    pallas_call x1, Pallas kernels: 65.9 us -> 61.2 us  [per_device(): pl.pallas_call(functools.partial(kernel, nx, nz, ny, docs), out_shape=[pl...]
    unnamed x4, local copies, waits for them, and re-layouts: 5.79 us -> 2.52 us
where the time goes in v3:
time: 65 us; the launch traced here: 64.3 us
  Pallas kernels  61.2 us (94%)
  local copies, waits for them, and re-layouts  2.52 us (4%)
    pallas_call x1, Pallas kernels, per_device(): pl.pallas_call(functools.partial(kernel, nx, nz, ny, docs), out_shape=[pl...  61.2 us
    unnamed x4, local copies, waits for them, and re-layouts  2.52 us

profile of v3, /device:TPU:24, one launch (start us, length us, event | category | flops | bytes accessed | tf_op | source)
XLA Modules:
  0.0 64.3 jit_solution(9150930709053194374)
XLA Ops:
  0.6 61.2 %shard_map.102 = (bf16[128,512]{1,0:T(8,128)(2,1)S(1)}, bf16[128,256]{1,0:T(8,128)(2,1)S(1)}, bf16[128,128]{1,0:T(8,128)(2,1)S(1)}, bf16[128,128]{1,0:T(8,128)(2,1)S(1)}) custom-call(bf16[128,256]{1,0:T(8,128)(2,1)} %q_hbm.1, bf16[128,128]{1,0:T(8,128)(2,1)} %k_hbm.1, bf16[128,128]{1,0:T(8,128)(2,1)} %v_hbm.1, bf16[256,4096]{1,0:T(8,128)(2,1)} %w_hbm.1, ...), custom_call_target="tpu_custom_call" | custom-call | flops 3758096384 | bytes 4194304 | tf_op jit(solution)/shard_map/pallas_call | solution.py:491
  61.8 0.7 %copy.15 = bf16[128,512]{1,0:T(8,128)(2,1)} copy(bf16[128,512]{1,0:T(8,128)(2,1)S(1)} %get-tuple-element.4) | data formatting | bytes 262144
  62.5 0.6 copy.17
  63.1 0.6 copy.18
  63.7 0.6 copy.16

commit v4 on v3

--- a/solution.py
+++ b/solution.py
@@ -141,8 +141,7 @@
         q_t[:, at128(x * HEADS + h)] = q_own[:, h * HD : (h + 1) * HD].T
     for d in range(1, nx):
         q_copy(d).start()
-    kv_start(0, 1)
-    kv_start(1, 3, 1)
+    kv_start(1, 3)
 
     load_order.wait()
     load_segment.wait()
@@ -212,14 +211,16 @@
     for d in range(1, nx):
         q_copy(d).wait_recv()
     kv_relay(1, 3, 6, 2, 4)
+    kv_start(0, 1)
+    kv_start(1, 1)
     score_blocks(z)
     score_far(3, wait=False)
-    score_far(1)
     cotangent_relay()
     kv_relay(0, 6, 5, 7, 8)
     score_far(6, wait=False)
     score_far(2)
     kv_relay(1, 6, 5, 7, 8)
+    score_far(1)
     cotangent()
     score_far(4, 5, 7)
     kv_wait(0, 8)
@@ -338,8 +339,6 @@
 
     grad_far(1, 5, 7)
     grad_antipode(1)
-    grad_far(1, 2, 4, 1, 6, 3)
-    dv_blocks(z)
     dq_t[...] = jnp.zeros_like(dq_t)
     for d in range(1, nx):
         in_copy(d).wait_recv()
@@ -348,11 +347,13 @@
     def dq_copy(d):
         return remote(dq_send.at[:, at256(x_at[d])], dq_recv.at[d], dq_s.at[d], dq_r.at[d], x_peer[d])
 
-    def pc_copy():
-        return remote(part_send, part_recv, pc_s.at[0], pc_r.at[0], partner)
+    far_first = sorted(range(1, ny), key=lambda d: -min(d, ny - d)) + [0]
+
+    def pc_copy(d):
+        return remote(part_send.at[d], part_recv.at[d], pc_s.at[d], pc_r.at[d], partner)
 
     def py_copy(d):
-        return remote(y_send.at[y_at[d]], y_recv.at[d], py_s.at[d], py_r.at[d], y_peer[d])
+        return remote(y_send.at[d], y_recv.at[d], py_s.at[d], py_r.at[d], y_peer[d])
 
     def project():
         for d in range(1, nx):
@@ -368,33 +369,22 @@
             attended.append(acc.astype(BF))
         attended = jnp.concatenate(attended, axis=0)
 
-        @pl.loop(0, ny)
-        def _(yp):
-            for c in range(2):
-                at = pl.ds(pl.multiple_of((yp * 2 + c) * features, features), features)
-                part = mm(attended, w[:, at], TN)
-
-                @pl.when(core == c)
-                def _():
-                    part_own[yp] = part
-
-                @pl.when(core != c)
-                def _():
-                    part_send[yp] = part.astype(BF)
-
-        pc_copy().start()
+        for d in far_first:
+            other = pl.ds(pl.multiple_of((y_at[d] * 2 + 1 - core) * features, features), features)
+            part_send[d] = mm(attended, w[:, other], TN).astype(BF)
+            pc_copy(d).start()
+            own = pl.ds(pl.multiple_of((y_at[d] * 2 + core) * features, features), features)
+            part_own[d] = mm(attended, w[:, own], TN)
 
     def spread():
-        pc_copy().wait_recv()
-
-        @pl.loop(0, ny)
-        def _(yp):
-            part = part_own[yp] + part_recv[yp].astype(F32)
-            part_own[yp] = part
-            y_send[yp] = part.astype(BF)
-
-        for d in range(1, ny):
-            py_copy(d).start()
+        for d in far_first:
+            pc_copy(d).wait_recv()
+            part = part_own[d] + part_recv[d].astype(F32)
+            if d == 0:
+                part_own[d] = part
+            else:
+                y_send[d] = part.astype(BF)
+                py_copy(d).start()
 
     def send_dq():
         for s in range(slots):
@@ -406,12 +396,15 @@
 
     grad_far(0, 5, 7)
     grad_antipode(0)
+    grad_far(1, 2, 4, 6)
     rs_hubs(1, 6)
     grad_far(0, 2, 4)
     project()
     grad_far(0, 6)
     rs_hubs(0, 6)
-    grad_far(0, 3, 1)
+    grad_far(1, 1, 3)
+    dv_blocks(z)
+    grad_far(0, 1, 3)
     ds_blocks(z)
     send_dq()
     spread()
@@ -436,7 +429,7 @@
         dq_v[:, h * 128 : (h + 1) * 128] = acc.T.astype(BF)
     for d in range(1, ny):
         py_copy(d).wait_recv()
-    out = part_own[y]
+    out = part_own[0]
     for d in range(1, ny):
         out = out + y_recv[d].astype(F32)
     out_v[...] = out.astype(BF)
@@ -455,7 +448,7 @@
         py_copy(d).wait_send()
     for d in range(ny):
         gc_copy(d).wait_send()
-    pc_copy().wait_send()
+        pc_copy(d).wait_send()
 
 
 def per_device(nx, nz, ny, docs, query, key_proj, value, out_weight, grad_out, order, segment):
@@ -485,7 +478,7 @@
         vm(ny, ROWS, features, dtype=F32), vm(ny, ROWS, features), vm(ny, ROWS, features),
         vm(ny, ROWS, features), vm(ny, ROWS, features),
         sem(7), sem(2, 17), sem(2, 17),
-    ] + [sem(nx)] * 12 + [sem(ny)] * 4 + [sem(1)] * 2 + [sem(ny)] * 2 + [sem(2, 17)] * 2
+    ] + [sem(nx)] * 12 + [sem(ny)] * 8 + [sem(2, 17)] * 2
     args = (query, key_proj, value, out_weight, grad_out, order, segment)
     flops = 2 * width * keys * HD * 6 + 4 * ROWS * HEADS * HD * out_weight.shape[1]
     return pl.pallas_call(

time: 65 us -> 63.4 us (0.975)
  Pallas kernels: 61.2 us -> 59.7 us
    pallas_call x1, Pallas kernels: 61.2 us -> 59.7 us  [per_device(): pl.pallas_call(functools.partial(kernel, nx, nz, ny, docs), out_shape=[pl...]
where the time goes in v4:
time: 63.4 us; the launch traced here: 62.9 us
  Pallas kernels  59.7 us (94%)
  local copies, waits for them, and re-layouts  2.52 us (4%)
  between operations  0.64 us (1%)
    pallas_call x1, Pallas kernels, per_device(): pl.pallas_call(functools.partial(kernel, nx, nz, ny, docs), out_shape=[pl...  59.7 us
    unnamed x4, local copies, waits for them, and re-layouts  2.52 us

profile of v4, /device:TPU:24, one launch (start us, length us, event | category | flops | bytes accessed | tf_op | source)
XLA Modules:
  0.0 62.9 jit_solution(8449455600594936989)
XLA Ops:
  0.6 59.7 %shard_map.102 = (bf16[128,512]{1,0:T(8,128)(2,1)S(1)}, bf16[128,256]{1,0:T(8,128)(2,1)S(1)}, bf16[128,128]{1,0:T(8,128)(2,1)S(1)}, bf16[128,128]{1,0:T(8,128)(2,1)S(1)}) custom-call(bf16[128,256]{1,0:T(8,128)(2,1)} %q_hbm.1, bf16[128,128]{1,0:T(8,128)(2,1)} %k_hbm.1, bf16[128,128]{1,0:T(8,128)(2,1)} %v_hbm.1, bf16[256,4096]{1,0:T(8,128)(2,1)} %w_hbm.1, ...), custom_call_target="tpu_custom_call" | custom-call | flops 3758096384 | bytes 4194304 | tf_op jit(solution)/shard_map/pallas_call | solution.py:484
  60.4 0.7 %copy.15 = bf16[128,512]{1,0:T(8,128)(2,1)} copy(bf16[128,512]{1,0:T(8,128)(2,1)S(1)} %get-tuple-element.4) | data formatting | bytes 262144
  61.0 0.6 copy.17
  61.6 0.6 copy.18
  62.3 0.6 %copy.16 = bf16[128,256]{1,0:T(8,128)(2,1)} copy(bf16[128,256]{1,0:T(8,128)(2,1)S(1)} %get-tuple-element.5) | data formatting | bytes 131072
